TPU v7x, 128 devices: a whole 4x4x4 slice. The times are simulated.
128 devices in a mesh: fsdp: 16 (over y, z), tp: 8 (over x, core).
Axes of the slice: x: 4, y: 4, z: 4, core: 2. Of those that a mesh axis runs over, the one named last changes fastest.
Arguments:
- tokens: bfloat16 [4096, 4096], P('fsdp', 'tp'), may hold values from -6 to 6
- gate_tiles: bfloat16 [288, 1024, 128], P('fsdp', 'tp'), may hold values from -0.125 to 0.125
- up_tiles: bfloat16 [288, 1024, 128], P('fsdp', 'tp'), may hold values from -0.125 to 0.125
- gate_slots: int32 [288, 8], P(None, 'tp'), may hold values from -1 to 27, as said below
- up_slots: int32 [288, 8], P(None, 'tp'), may hold values from -1 to 27, as said below
- cotangent: bfloat16 [4096, 14336], P('fsdp', 'tp'), may hold values from -6 to 6
Outputs:
- hidden: bfloat16 [4096, 14336], P('fsdp', 'tp')
- input_grad: bfloat16 [4096, 4096], P('fsdp', 'tp')
- gate_tile_grad: bfloat16 [288, 1024, 128], P('fsdp', 'tp')
- up_tile_grad: bfloat16 [288, 1024, 128], P('fsdp', 'tp')
Inputs may be any that keep to these rules, and one draw needn't show every extreme that they name: `gate_slots`: for each owner (rows f * 18 to (f + 1) * 18 - 1, column t) the non-negative entries are distinct positions of that owner, stand before its -1 entries, and number 10 to 18; in every draw some owner fills all 18 slots. `up_slots`: as for gate_slots, drawn independently.
All inputs are finite; a program needn't handle non-finite values.
Results may differ from a plain program's by a relative error of at most 0.02.
Values may be sent and summed in bfloat16 or wider, within the bound.
No kernel may reach another device: no remote copies, remote signals or barrier semaphores. Data moves between devices by JAX's collectives and lax.ppermute only.
A program may use at most 192 MiB of HBM per device.

v0:
```python
import jax
import jax.numpy as jnp
from jax import lax
from jax.sharding import PartitionSpec as P


def per_device(tokens, gate_tiles, up_tiles, gate_slots, up_slots, cotangent):
    n_fsdp = lax.axis_size("fsdp")
    n_tp = lax.axis_size("tp")
    tile_size = gate_tiles.shape[-1]
    capacity = gate_tiles.shape[0]
    tok_rows = tokens.shape[0]
    gathered = lax.all_gather(tokens, "tp", axis=1, tiled=True)
    model_width = gathered.shape[1]
    ff_local = cotangent.shape[1]
    row_tiles = model_width // (tile_size * n_fsdp)
    col_tiles = ff_local // tile_size
    owner_tiles = row_tiles * col_tiles
    positions = jnp.arange(owner_tiles, dtype=jnp.int32)
    gate_table = gate_slots.reshape(n_fsdp, capacity)
    up_table = up_slots.reshape(n_fsdp, capacity)

    def selector(table, kind):
        picks = (table[:, :, None] == positions).astype(kind)
        return picks.reshape(table.shape[0], table.shape[1], row_tiles, col_tiles)

    gate_select = selector(gate_table, jnp.bfloat16)
    up_select = selector(up_table, jnp.bfloat16)
    gate_all, up_all = (
        lax.all_gather(gate_tiles, "fsdp", axis=0, tiled=True),
        lax.all_gather(up_tiles, "fsdp", axis=0, tiled=True),
    )

    def unpack(blocks, select):
        dense_tiles = jnp.einsum(
            "fcrj,fcab->frjab",
            select,
            blocks.reshape(n_fsdp, capacity, tile_size, tile_size),
            preferred_element_type=jnp.float32,
        )
        return dense_tiles.astype(jnp.bfloat16)

    w_gate = unpack(gate_all, gate_select)
    w_up = unpack(up_all, up_select)
    token_view = gathered.reshape(tok_rows, n_fsdp, row_tiles, tile_size)
    gate = jnp.einsum(
        "tfra,frjab->tjb", token_view, w_gate, preferred_element_type=jnp.float32
    ).reshape(tok_rows, ff_local)
    up = jnp.einsum(
        "tfra,frjab->tjb", token_view, w_up, preferred_element_type=jnp.float32
    ).reshape(tok_rows, ff_local)
    sigmoid_gate = jax.nn.sigmoid(gate)
    activated = gate * sigmoid_gate
    hidden = (activated * up).astype(jnp.bfloat16)
    upstream = cotangent.astype(jnp.float32)
    gate_grad = (upstream * up * sigmoid_gate * (1.0 + gate * (1.0 - sigmoid_gate))).astype(
        jnp.bfloat16
    )
    up_grad = (upstream * activated).astype(jnp.bfloat16)
    gate_view = gate_grad.reshape(tok_rows, col_tiles, tile_size)
    up_view = up_grad.reshape(tok_rows, col_tiles, tile_size)
    total = jnp.einsum(
        "frjab,tjb->frat", w_gate, gate_view, preferred_element_type=jnp.float32
    ) + jnp.einsum("frjab,tjb->frat", w_up, up_view, preferred_element_type=jnp.float32)
    input_part = lax.psum_scatter(
        total.reshape(model_width // n_tp * lax.axis_size("tp"), tok_rows).astype(jnp.bfloat16),
        "tp",
        scatter_dimension=0,
        tiled=True,
    ).astype(jnp.float32)
    input_grad = input_part.T.astype(jnp.bfloat16)
    gate_dense = jnp.einsum(
        "tfra,tjb->frajb", token_view, gate_view, preferred_element_type=jnp.float32
    ).astype(jnp.bfloat16)
    up_dense = jnp.einsum(
        "tfra,tjb->frajb", token_view, up_view, preferred_element_type=jnp.float32
    ).astype(jnp.bfloat16)
    gate_packed = jnp.einsum(
        "fcrj,frajb->fcab", gate_select, gate_dense, preferred_element_type=jnp.float32
    )
    up_packed = jnp.einsum(
        "fcrj,frajb->fcab", up_select, up_dense, preferred_element_type=jnp.float32
    )
    gate_packed = gate_packed.reshape(capacity * lax.axis_size("fsdp"), tile_size, tile_size)
    up_packed = up_packed.reshape(capacity * lax.axis_size("fsdp"), tile_size, tile_size)
    summed = lax.psum_scatter(
        jnp.concatenate([gate_packed, up_packed], axis=2).astype(jnp.bfloat16),
        "fsdp",
        scatter_dimension=0,
        tiled=True,
    ).astype(jnp.float32)
    gate_tile_grad = summed[:, :, :tile_size].astype(jnp.bfloat16)
    up_tile_grad = summed[:, :, tile_size:].astype(jnp.bfloat16)
    return (hidden, input_grad, gate_tile_grad, up_tile_grad)


def solution(mesh):
    placed = (
        P("fsdp", "tp"),
        P("fsdp", "tp", None),
        P("fsdp", "tp", None),
        P(None, "tp"),
        P(None, "tp"),
        P("fsdp", "tp"),
    )
    return jax.shard_map(
        per_device,
        mesh=mesh,
        in_specs=placed,
        out_specs=(P("fsdp", "tp"), P("fsdp", "tp"), P("fsdp", "tp", None), P("fsdp", "tp", None)),
        check_vma=False,
    )
```

profile of v0, /device:TPU:0, one launch (start us, length us, event | category | flops | bytes accessed | tf_op | source)
XLA Modules:
  0.0 513.8 jit_solution(2433849524178457601)
XLA Ops:
  7.2 0.7 all-gather.4.cloned.1.call-update
  7.9 1.8 copy.60
  9.8 0.7 all-gather.8.cloned.1.call-update
  10.5 0.7 reduce
  11.2 0.7 reduce.1
  11.9 0.1 eq.49
  12.1 2.2 copy.67
  14.3 74.0 %all-gather.4.cloned.1.call-done = bf16[288,128,128]{2,1,0:T(8,128)(2,1)} async-done(((bf16[18,128,128]{2,1,0:T(8,128)(2,1)}), bf16[288,128,128]{2,1,0:T(8,128)(2,1)}) %all-gather.4.cloned.1.call-update) | async-done | bytes 9437200 | tf_op jit(solution)/shard_map/all_gather | solution.py:30
  88.4 16.0 %fusion.2 = bf16[16,2,14,128,128]{4,2,3,1,0:T(8,128)(2,1)} fusion(bf16[16,18,128,128,1]{3,2,1,0,4:T(8,128)(2,1)} %bitcast.119, s32[2,14]{1,0:T(2,128)S(1)} %multiply_add_fusion, s32[16,18]{1,0:T(8,128)S(1)} %eq.42), kind=kOutput, calls=%fused_computation.9 | convolution fusion | flops 264249216 | bytes 24118512 | tf_op jit(solution)/shard_map/fcrj,fcab->frjab/dot_general | solution.py:35
  104.4 11.0 %all-gather.6.cloned.1.call-done = bf16[256,4096]{0,1:T(8,128)(2,1)} async-done(((bf16[256,512]{0,1:T(8,128)(2,1)}), bf16[256,4096]{0,1:T(8,128)(2,1)}) %all-gather.6.cloned.1.call-update) | async-done | bytes 2097168 | tf_op jit(solution)/shard_map/all_gather | solution.py:13
  115.4 14.4 %fusion.6 = f32[14,128,256,1,1]{2,1,0,4,3:T(8,128)} fusion(bf16[256,16,2,128,1]{0,3,4,2,1:T(8,128)(2,1)} %bitcast.121, bf16[16,2,14,128,128]{4,2,3,1,0:T(8,128)(2,1)} %fusion.2), kind=kOutput, calls=%fused_computation.14 | convolution fusion | flops 3758096384 | bytes 18612224 | tf_op jit(solution)/shard_map/tfra,frjab->tjb/dot_general | solution.py:46
  129.8 63.8 %all-gather.8.cloned.1.call-done = bf16[288,128,128]{2,1,0:T(8,128)(2,1)} async-done(((bf16[18,128,128]{2,1,0:T(8,128)(2,1)}), bf16[288,128,128]{2,1,0:T(8,128)(2,1)}) %all-gather.8.cloned.1.call-update) | async-done | bytes 9437200 | tf_op jit(solution)/shard_map/all_gather | solution.py:31
  193.6 15.7 %fusion = bf16[16,2,14,128,128]{4,2,3,1,0:T(8,128)(2,1)} fusion(bf16[16,18,128,128,1]{3,2,1,0,4:T(8,128)(2,1)} %bitcast.120, s32[16,18]{1,0:T(8,128)S(1)} %eq.49, s32[2,14]{1,0:T(2,128)S(1)} %multiply_add_fusion), kind=kOutput, calls=%fused_computation.7 | convolution fusion | flops 264249216 | bytes 24118512 | tf_op jit(solution)/shard_map/fcrj,fcab->frjab/dot_general | solution.py:35
  209.4 13.6 %fusion.8 = f32[14,128,256,1,1]{2,1,0,4,3:T(8,128)S(1)} fusion(bf16[256,16,2,128,1]{0,3,4,2,1:T(8,128)(2,1)S(1)} %bitcast.122, bf16[16,2,14,128,128]{4,2,3,1,0:T(8,128)(2,1)} %fusion), kind=kOutput, calls=%fused_computation.16 | convolution fusion | flops 3758096384 | bytes 18612224 | tf_op jit(solution)/shard_map/tfra,frjab->tjb/dot_general | solution.py:49
  223.0 2.4 fusion.11
  225.3 7.2 %convert_bitcast_fusion = bf16[16,2,128,14,128]{2,4,1,0,3:T(8,128)(2,1)} fusion(bf16[256,14,128,1,1]{0,2,4,3,1:T(8,128)(2,1)S(1)} %bitcast.125, bf16[256,16,2,128,1]{0,3,2,1,4:T(8,128)(2,1)S(1)} %bitcast.123), kind=kOutput, calls=%fused_computation.5 | convolution fusion | flops 3765436416 | bytes 17694720 | tf_op jit(solution)/shard_map/tfra,tjb->frajb/dot_general | solution.py:75
  232.5 24.7 %copy.75 = bf16[16,2,128,14,128]{4,3,1,2,0:T(8,128)(2,1)} copy(bf16[16,2,128,14,128]{2,4,1,0,3:T(8,128)(2,1)} %convert_bitcast_fusion) | data formatting | bytes 29360128 | tf_op jit(solution)/shard_map/convert_element_type | solution.py:77
  257.2 10.2 %bitcast_convert_fusion = bf16[16,18,128,128]{3,1,2,0:T(8,128)(2,1)} fusion(bf16[16,2,128,14,128]{4,3,1,2,0:T(8,128)(2,1)} %copy.75, s32[16,18]{1,0:T(8,128)S(1)} %eq.49, s32[2,14]{1,0:T(2,128)S(1)} %multiply_add_fusion), kind=kOutput, calls=%fused_computation.2 | convolution fusion | flops 268967808 | bytes 24118512 | tf_op jit(solution)/shard_map/fcrj,frajb->fcab/dot_general | solution.py:81
  267.5 11.0 %copy.76 = bf16[16,18,128,128]{3,2,1,0:T(8,128)(2,1)} copy(bf16[16,18,128,128]{3,1,2,0:T(8,128)(2,1)} %bitcast_convert_fusion) | data formatting | bytes 18874368 | tf_op jit(solution)/shard_map/convert.4
  278.4 8.6 %convert_bitcast_fusion.1 = bf16[16,2,128,14,128]{2,4,1,0,3:T(8,128)(2,1)} fusion(bf16[256,14,128,1,1]{0,2,4,3,1:T(8,128)(2,1)} %bitcast.127, bf16[256,16,2,128,1]{0,3,2,1,4:T(8,128)(2,1)S(1)} %bitcast.124), kind=kOutput, calls=%fused_computation.6 | convolution fusion | flops 3765436416 | bytes 17694720 | tf_op jit(solution)/shard_map/tfra,tjb->frajb/dot_general | solution.py:72
  287.1 24.7 %copy.72 = bf16[16,2,128,14,128]{4,3,1,2,0:T(8,128)(2,1)} copy(bf16[16,2,128,14,128]{2,4,1,0,3:T(8,128)(2,1)} %convert_bitcast_fusion.1) | data formatting | bytes 29360128 | tf_op jit(solution)/shard_map/convert_element_type | solution.py:74
  311.8 10.4 %bitcast_convert_fusion.1 = bf16[16,18,128,128]{3,1,2,0:T(8,128)(2,1)} fusion(bf16[16,2,128,14,128]{4,3,1,2,0:T(8,128)(2,1)} %copy.72, s32[2,14]{1,0:T(2,128)S(1)} %multiply_add_fusion, s32[16,18]{1,0:T(8,128)S(1)} %eq.42), kind=kOutput, calls=%fused_computation.3 | convolution fusion | flops 268967808 | bytes 24118512 | tf_op jit(solution)/shard_map/fcrj,frajb->fcab/dot_general | solution.py:78
  322.2 11.0 %copy.73 = bf16[16,18,128,128]{3,2,1,0:T(8,128)(2,1)} copy(bf16[16,18,128,128]{3,1,2,0:T(8,128)(2,1)} %bitcast_convert_fusion.1) | data formatting | bytes 18874368 | tf_op jit(solution)/shard_map/convert.5
  333.2 16.8 %pad_maximum_fusion = bf16[288,128,256]{2,1,0:T(8,128)(2,1)} fusion(bf16[288,128,128]{2,1,0:T(8,128)(2,1)} %bitcast.117, bf16[288,128,128]{2,1,0:T(8,128)(2,1)} %bitcast.118), kind=kLoop, calls=%fused_computation.4 | loop fusion | flops 37748736 | bytes 37748736 | tf_op jit(solution)/shard_map/concatenate | solution.py:87
  350.1 1.1 copy-done.1
  351.2 9.3 %fusion.5 = f32[16,2,128,256,1]{3,2,4,1,0:T(8,128)S(1)} fusion(bf16[256,14,128,1,1]{0,2,1,4,3:T(8,128)(2,1)S(1)} %bitcast.128, bf16[16,2,14,128,128]{4,2,3,1,0:T(8,128)(2,1)} %fusion.2), kind=kOutput, calls=%fused_computation.13 | convolution fusion | flops 3758096384 | bytes 19791872 | tf_op jit(solution)/shard_map/frjab,tjb->frat/dot_general | solution.py:62
  360.5 10.7 %fusion.4 = bf16[16,2,128,256]{3,2,1,0:T(8,128)(2,1)} fusion(f32[16,2,128,256,1]{3,2,4,1,0:T(8,128)S(1)} %fusion.5, bf16[256,14,128,1,1]{0,2,1,4,3:T(8,128)(2,1)S(1)} %bitcast.126, bf16[16,2,14,128,128]{4,2,3,1,0:T(8,128)(2,1)} %fusion), kind=kOutput, calls=%fused_computation.12 | convolution fusion | flops 3760193536 | bytes 21889024 | tf_op jit(solution)/shard_map/frjab,tjb->frat/dot_general | solution.py:64
  371.2 4.1 copy.70
  375.3 1.4 copy.77
  376.7 94.2 %reduce-scatter.5.cloned.1.call-done = bf16[18,128,256]{2,1,0:T(8,128)(2,1)} async-done(((bf16[288,128,256]{2,1,0:T(8,128)(2,1)}), bf16[18,128,256]{2,1,0:T(8,128)(2,1)}) %reduce-scatter.5.cloned.1.call-update) | async-done | bytes 1179664 | tf_op jit(solution)/shard_map/reduce_scatter | solution.py:86
  470.9 2.4 fusion.26
  473.3 33.8 %reduce-scatter.3.cloned.1.call-done = bf16[512,256]{0,1:T(8,128)(2,1)} async-done(((bf16[4096,256]{0,1:T(8,128)(2,1)}), bf16[512,256]{0,1:T(8,128)(2,1)}) %reduce-scatter.3.cloned.1.call-update) | async-done | bytes 262160 | tf_op jit(solution)/shard_map/reduce_scatter | solution.py:65
  (19 shorter events, 0.4 us)
Async XLA Ops:
  7.2 81.2 %all-gather.4.cloned.1.call-start = ((), (), s32[]{:S(2)}) async-start(), calls=%async_computation.2 | async-start | bytes 10027008 | tf_op jit(solution)/shard_map/all_gather | solution.py:30
  7.9 107.5 %all-gather.6.cloned.1.call-start = ((), (), s32[]{:S(2)}) async-start(), calls=%async_computation.3 | async-start | bytes 2359296 | tf_op jit(solution)/shard_map/all_gather | solution.py:13
  9.8 183.9 %all-gather.8.cloned.1.call-start = ((), (), s32[]{:S(2)}) async-start(), calls=%async_computation.4 | async-start | bytes 10027008 | tf_op jit(solution)/shard_map/all_gather | solution.py:31
  10.5 460.4 %reduce-scatter.5.cloned.1.call-start = ((), (), s32[]{:S(2)}) async-start(), calls=%async_computation.6 | async-start | bytes 20054016 | tf_op jit(solution)/shard_map/reduce_scatter | solution.py:86
  193.6 15.7 %copy-start = (bf16[256,4096]{0,1:T(8,128)(2,1)S(1)}, bf16[256,4096]{0,1:T(8,128)(2,1)}, u32[]{:S(2)}) copy-start(bf16[256,4096]{0,1:T(8,128)(2,1)} %all-gather.6.cloned.1.call-done) | copy-start | bytes 6291460
  209.4 13.6 %copy-start.3 = (bf16[256,1792]{0,1:T(8,128)(2,1)S(1)}, bf16[256,1792]{0,1:T(8,128)(2,1)}, u32[]{:S(2)}) copy-start(bf16[256,1792]{0,1:T(8,128)(2,1)} %copy.67) | copy-start | bytes 2752516
  209.4 13.6 %copy-start.4 = (f32[14,128,256,1,1]{2,1,0,4,3:T(8,128)S(1)}, f32[14,128,256,1,1]{2,1,0,4,3:T(8,128)}, u32[]{:S(2)}) copy-start(f32[14,128,256,1,1]{2,1,0,4,3:T(8,128)} %fusion.6) | copy-start | bytes 5505028
  350.0 1.2 copy-start.1
  350.0 157.1 %reduce-scatter.3.cloned.1.call-start = ((), (), s32[]{:S(2)}) async-start(), calls=%async_computation.5 | async-start | bytes 2359296 | tf_op jit(solution)/shard_map/reduce_scatter | solution.py:65
  360.5 14.9 %copy-start.2 = (bf16[256,1792]{0,1:T(8,128)(2,1)S(1)}, bf16[256,1792]{0,1:T(8,128)(2,1)}, u32[]{:S(2)}) copy-start(bf16[256,1792]{0,1:T(8,128)(2,1)} %get-tuple-element.17) | copy-start | bytes 2752516
Sparse Core Ops, SparseCore 0:
  10.2 78.1 all-gather.3
  90.7 24.6 all-gather.5
  117.6 75.9 all-gather.7
  350.1 120.7 reduce-scatter.4
  473.8 33.2 reduce-scatter.2
where the time goes:
time: 520 us; the launch traced here: 514 us
  waiting for transfers between devices  278 us (53%)
  matrix products  116 us (22%)
  local copies, waits for them, and re-layouts  84.6 us (16%)
  other arithmetic  20.6 us (4%)
  between operations  14.1 us (3%)
    reduce_scatter x1, waiting for transfers between devices, per_device(): lax.psum_scatter(jnp.concatenate([gate_packed, up_packed], axis=2).astype...  94.2 us
    all_gather x1, waiting for transfers between devices, per_device(): lax.all_gather(gate_tiles, 'fsdp', axis=0, tiled=True)  74 us
    all_gather x1, waiting for transfers between devices, per_device(): lax.all_gather(up_tiles, 'fsdp', axis=0, tiled=True)  63.8 us
    reduce_scatter x1, waiting for transfers between devices, per_device(): lax.psum_scatter(total.reshape(model_width // n_tp * lax.axis_size('tp'),...  33.8 us
    dot_general x2, matrix products, unpack(): jnp.einsum('fcrj,fcab->frjab', select, blocks.reshape(n_fsdp, capacity, t...  31.8 us
    convert_element_type x1, local copies, waits for them, and re-layouts, per_device(): up_dense = jnp.einsum('tfra,tjb->frajb', token_view, up_view, preferred_e...  24.7 us
    convert_element_type x1, local copies, waits for them, and re-layouts, per_device(): gate_dense = jnp.einsum('tfra,tjb->frajb', token_view, gate_view, preferr...  24.7 us
    another operation x2, local copies, waits for them, and re-layouts  21.9 us
  transfers between devices with their start and end apart: 5, of which 5 were waited for; matrix products, arithmetic and copies ran while one was open for 12% of the time, Pallas kernels for 0%

commit v1 on v0

--- a/solution.py
+++ b/solution.py
@@ -1,7 +1,31 @@
+import functools
 import jax
 import jax.numpy as jnp
 from jax import lax
 from jax.sharding import PartitionSpec as P
+
+
+def clear_seats_all(array_here, comm_axis):
+    panels = []
+    n_peers_all = jax.lax.axis_size(comm_axis)
+    for pp in [*range(n_peers_all)]:
+        panels.append((pp, (pp + 1) % n_peers_all))
+
+    def deliver_seats_all_on(p_next):
+        if len(p_next) == n_peers_all:
+            return p_next
+        return deliver_seats_all_on(
+            [jax.lax.ppermute(p_next[0], axis_name=comm_axis, perm=panels), *p_next]
+        )
+
+    return jnp.roll(
+        jnp.concatenate(deliver_seats_all_on([array_here]), axis=1),
+        shift=(jax.lax.axis_index(comm_axis) + 1) * array_here.shape[1],
+        axis=1,
+    )
+
+
+_follow_words = functools.partial(clear_seats_all, comm_axis="tp")
 
 
 def per_device(tokens, gate_tiles, up_tiles, gate_slots, up_slots, cotangent):
@@ -10,7 +34,7 @@
     tile_size = gate_tiles.shape[-1]
     capacity = gate_tiles.shape[0]
     tok_rows = tokens.shape[0]
-    gathered = lax.all_gather(tokens, "tp", axis=1, tiled=True)
+    gathered = _follow_words(tokens)
     model_width = gathered.shape[1]
     ff_local = cotangent.shape[1]
     row_tiles = model_width // (tile_size * n_fsdp)

time: 520 us -> 498 us (0.958)
  waiting for transfers between devices: 278 us -> 247 us
  matrix products: 116 us -> 129 us
    ppermute x0 -> x7, waiting for transfers between devices: none -> 47.4 us  [deliver_seats_all_on(): jax.lax.ppermute(p_next[0], axis_name=comm_axis, perm=panels)]
    dot_general x0 -> x2, local copies, waits for them, and re-layouts: none -> 47.4 us  [the longest x1 24.4 us: per_device(): jnp.einsum('tfra,frjab->tjb', token_view, w_gate, preferred_element_type=...]
    convert_element_type x2, local copies, waits for them, and re-layouts: 49.4 us -> 2.75 us  [the longest x1 1.45 us: per_device(): (upstream * up * sigmoid_gate * (1.0 + gate * (1.0 - sigmoid_gate))).asty...]
    all_gather x1, waiting for transfers between devices: 74 us -> 28.9 us  [per_device(): lax.all_gather(gate_tiles, 'fsdp', axis=0, tiled=True)]
    all_gather x1, waiting for transfers between devices: 63.8 us -> 37.5 us  [per_device(): lax.all_gather(up_tiles, 'fsdp', axis=0, tiled=True)]
    all_gather x1 -> x0, waiting for transfers between devices: 11 us -> none  [per_device(): gathered = lax.all_gather(tokens, 'tp', axis=1, tiled=True)]
    dot_general x1, matrix products: 10.2 us -> 18.2 us  [per_device(): jnp.einsum('fcrj,frajb->fcab', up_select, up_dense, preferred_element_typ...]
    dot_general x1, matrix products: 10.4 us -> 18.2 us  [per_device(): jnp.einsum('fcrj,frajb->fcab', gate_select, gate_dense, preferred_element...]
  transfers between devices with their start and end apart: 5 -> 11, of which waited for: 5 -> 11; matrix products, arithmetic and copies ran while one was open for 12% -> 14% of each run, Pallas kernels for 0% -> 0%
where the time goes in v1:
time: 498 us; the launch traced here: 488 us
  waiting for transfers between devices  247 us (50%)
  matrix products  129 us (26%)
  local copies, waits for them, and re-layouts  80.2 us (16%)
  other arithmetic  18.2 us (4%)
  between operations  14.2 us (3%)
    reduce_scatter x1, waiting for transfers between devices, per_device(): lax.psum_scatter(jnp.concatenate([gate_packed, up_packed], axis=2).astype...  97.7 us
    ppermute x7, waiting for transfers between devices, deliver_seats_all_on(): jax.lax.ppermute(p_next[0], axis_name=comm_axis, perm=panels)  47.4 us
    all_gather x1, waiting for transfers between devices, per_device(): lax.all_gather(up_tiles, 'fsdp', axis=0, tiled=True)  37.5 us
    reduce_scatter x1, waiting for transfers between devices, per_device(): lax.psum_scatter(total.reshape(model_width // n_tp * lax.axis_size('tp'),...  33.7 us
    dot_general x2, matrix products, unpack(): jnp.einsum('fcrj,fcab->frjab', select, blocks.reshape(n_fsdp, capacity, t...  31.2 us
    all_gather x1, waiting for transfers between devices, per_device(): lax.all_gather(gate_tiles, 'fsdp', axis=0, tiled=True)  28.9 us
    dot_general x1, local copies, waits for them, and re-layouts, per_device(): jnp.einsum('tfra,frjab->tjb', token_view, w_gate, preferred_element_type=...  24.4 us
    dot_general x1, local copies, waits for them, and re-layouts, per_device(): jnp.einsum('tfra,frjab->tjb', token_view, w_up, preferred_element_type=jn...  23 us
  transfers between devices with their start and end apart: 11, of which 11 were waited for; matrix products, arithmetic and copies ran while one was open for 14% of the time, Pallas kernels for 0%

profile of v1, /device:TPU:0, one launch (start us, length us, event | category | flops | bytes accessed | tf_op | source)
XLA Modules:
  0.0 488.2 jit_solution(7904106828909276050)
XLA Ops:
  8.7 1.1 copy.37
  9.8 7.0 %collective-permute-done = bf16[256,512]{0,1:T(8,128)(2,1)S(1)} collective-permute-done((bf16[256,512]{0,1:T(8,128)(2,1)S(1)}, bf16[256,512]{0,1:T(8,128)(2,1)S(1)}, u32[]{:S(2)}, u32[]{:S(2)}) %collective-permute-start) | collective-permute-done | bytes 262176 | tf_op jit(solution)/shard_map/ppermute | solution.py:18
  16.8 7.0 %collective-permute-done.1 = bf16[256,512]{0,1:T(8,128)(2,1)S(1)} collective-permute-done((bf16[256,512]{0,1:T(8,128)(2,1)S(1)}, bf16[256,512]{0,1:T(8,128)(2,1)S(1)}, u32[]{:S(2)}, u32[]{:S(2)}) %collective-permute-start.1) | collective-permute-done | bytes 262176 | tf_op jit(solution)/shard_map/ppermute | solution.py:18
  23.8 7.0 %collective-permute-done.2 = bf16[256,512]{0,1:T(8,128)(2,1)S(1)} collective-permute-done((bf16[256,512]{0,1:T(8,128)(2,1)S(1)}, bf16[256,512]{0,1:T(8,128)(2,1)S(1)}, u32[]{:S(2)}, u32[]{:S(2)}) %collective-permute-start.2) | collective-permute-done | bytes 262176 | tf_op jit(solution)/shard_map/ppermute | solution.py:18
  30.8 7.0 %collective-permute-done.3 = bf16[256,512]{0,1:T(8,128)(2,1)S(1)} collective-permute-done((bf16[256,512]{0,1:T(8,128)(2,1)S(1)}, bf16[256,512]{0,1:T(8,128)(2,1)S(1)}, u32[]{:S(2)}, u32[]{:S(2)}) %collective-permute-start.3) | collective-permute-done | bytes 262176 | tf_op jit(solution)/shard_map/ppermute | solution.py:18
  37.8 7.0 %collective-permute-done.4 = bf16[256,512]{0,1:T(8,128)(2,1)S(1)} collective-permute-done((bf16[256,512]{0,1:T(8,128)(2,1)S(1)}, bf16[256,512]{0,1:T(8,128)(2,1)S(1)}, u32[]{:S(2)}, u32[]{:S(2)}) %collective-permute-start.4) | collective-permute-done | bytes 262176 | tf_op jit(solution)/shard_map/ppermute | solution.py:18
  44.8 7.0 %collective-permute-done.5 = bf16[256,512]{0,1:T(8,128)(2,1)S(1)} collective-permute-done((bf16[256,512]{0,1:T(8,128)(2,1)S(1)}, bf16[256,512]{0,1:T(8,128)(2,1)S(1)}, u32[]{:S(2)}, u32[]{:S(2)}) %collective-permute-start.5) | collective-permute-done | bytes 262176 | tf_op jit(solution)/shard_map/ppermute | solution.py:18
  53.4 5.4 %collective-permute-done.6 = bf16[256,512]{0,1:T(8,128)(2,1)S(1)} collective-permute-done((bf16[256,512]{0,1:T(8,128)(2,1)S(1)}, bf16[256,512]{0,1:T(8,128)(2,1)S(1)}, u32[]{:S(2)}, u32[]{:S(2)}) %collective-permute-start.6) | collective-permute-done | bytes 262176 | tf_op jit(solution)/shard_map/ppermute | solution.py:18
  59.4 28.9 %all-gather.3.cloned.1.call-done = bf16[288,128,128]{2,1,0:T(8,128)(2,1)} async-done(((bf16[18,128,128]{2,1,0:T(8,128)(2,1)}), bf16[288,128,128]{2,1,0:T(8,128)(2,1)}) %all-gather.3.cloned.1.call-update) | async-done | bytes 9437200 | tf_op jit(solution)/shard_map/all_gather | solution.py:54
  88.4 15.6 %fusion.12 = bf16[16,2,14,128,128]{4,2,3,1,0:T(8,128)(2,1)} fusion(bf16[16,18,128,128,1]{3,2,1,0,4:T(8,128)(2,1)} %bitcast.83, s32[2,14]{1,0:T(2,128)S(1)} %multiply_add_fusion, s32[16,18]{1,0:T(8,128)S(1)} %eq.45), kind=kOutput, calls=%fused_computation.15 | convolution fusion | flops 271589248 | bytes 24118512 | tf_op jit(solution)/shard_map/fcrj,fcab->frjab/dot_general | solution.py:59
  104.0 24.4 %copy.82 = bf16[14,128,128,16,2]{2,1,0,4,3:T(8,128)(2,1)} copy(bf16[14,128,128,16,2]{1,0,2,4,3:T(8,128)(2,1)} %bitcast.79) | data formatting | bytes 29360128 | tf_op jit(solution)/shard_map/tfra,frjab->tjb/dot_general | solution.py:70
  128.3 37.5 %all-gather.5.cloned.1.call-done = bf16[288,128,128]{2,1,0:T(8,128)(2,1)} async-done(((bf16[18,128,128]{2,1,0:T(8,128)(2,1)}), bf16[288,128,128]{2,1,0:T(8,128)(2,1)}) %all-gather.5.cloned.1.call-update) | async-done | bytes 9437200 | tf_op jit(solution)/shard_map/all_gather | solution.py:55
  165.9 15.6 %fusion.15 = bf16[16,2,14,128,128]{4,2,3,1,0:T(8,128)(2,1)} fusion(bf16[16,18,128,128,1]{3,2,1,0,4:T(8,128)(2,1)} %bitcast.84, s32[16,18]{1,0:T(8,128)S(1)} %eq.52, s32[2,14]{1,0:T(2,128)S(1)} %multiply_add_fusion), kind=kOutput, calls=%fused_computation.16 | convolution fusion | flops 271589248 | bytes 24118512 | tf_op jit(solution)/shard_map/fcrj,fcab->frjab/dot_general | solution.py:59
  181.4 23.0 %copy.85 = bf16[14,128,128,16,2]{2,1,0,4,3:T(8,128)(2,1)} copy(bf16[14,128,128,16,2]{1,0,2,4,3:T(8,128)(2,1)} %bitcast.80) | data formatting | bytes 29360128 | tf_op jit(solution)/shard_map/tfra,frjab->tjb/dot_general | solution.py:73
  204.5 9.1 %convolution_bitcast_fusion.1 = f32[256,1792]{1,0:T(8,128)} fusion(bf16[256,16,2,128]{0,3,2,1:T(8,128)(2,1)S(1)} %bitcast.85, bf16[1792,128,16,2]{1,0,3,2:T(8,128)(2,1)} %bitcast.89), kind=kOutput, calls=%fused_computation.22 | convolution fusion | flops 3758096384 | bytes 18612224 | tf_op jit(solution)/shard_map/tfra,frjab->tjb/dot_general | solution.py:70
  213.6 16.7 %fusion.27 = (bf16[256,1792]{1,0:T(8,128)(2,1)}, bf16[256,1792]{1,0:T(8,128)(2,1)}, bf16[256,1792]{1,0:T(8,128)(2,1)S(1)}) fusion(bf16[256,1792]{1,0:T(8,128)(2,1)} %param.11, f32[256,1792]{1,0:T(8,128)} %convolution_bitcast_fusion.1, bf16[256,16,2,128]{0,3,2,1:T(8,128)(2,1)S(1)} %bitcast.86, bf16[1792,128,16,2]{1,0,3,2:T(8,128)(2,1)} %bitcast.90), kind=kOutput, calls=%fused_computation.27 | convolution fusion | flops 3765436416 | bytes 22282240 | tf_op jit(solution)/shard_map/tfra,frjab->tjb/dot_general | solution.py:73
  230.2 1.3 copy.51
  231.5 1.5 copy.48
  233.0 8.4 %convolution_convert_fusion = bf16[16,2,128,14,128]{4,2,3,1,0:T(8,128)(2,1)} fusion(bf16[256,16,2,128,1]{0,3,4,2,1:T(8,128)(2,1)S(1)} %bitcast.87, bf16[256,14,128,1,1]{0,2,1,4,3:T(8,128)(2,1)} %bitcast.93), kind=kOutput, calls=%fused_computation.17 | convolution fusion | flops 3765436416 | bytes 17694720 | tf_op jit(solution)/shard_map/tfra,tjb->frajb/dot_general | solution.py:99
  241.4 18.2 %bitcast_convert_fusion = bf16[16,18,128,128]{3,1,2,0:T(8,128)(2,1)} fusion(bf16[16,2,128,14,128]{4,2,3,1,0:T(8,128)(2,1)} %convolution_convert_fusion, s32[16,18]{1,0:T(8,128)S(1)} %eq.52, s32[2,14]{1,0:T(2,128)S(1)} %multiply_add_fusion), kind=kOutput, calls=%fused_computation | convolution fusion | flops 268967808 | bytes 24118512 | tf_op jit(solution)/shard_map/fcrj,frajb->fcab/dot_general | solution.py:105
  259.6 11.0 %copy.60 = bf16[16,18,128,128]{3,2,1,0:T(8,128)(2,1)} copy(bf16[16,18,128,128]{3,1,2,0:T(8,128)(2,1)} %bitcast_convert_fusion) | data formatting | bytes 18874368 | tf_op jit(solution)/shard_map/convert.4
  270.6 7.7 %convolution_convert_fusion.1 = bf16[16,2,128,14,128]{4,2,3,1,0:T(8,128)(2,1)} fusion(bf16[256,16,2,128,1]{0,3,4,2,1:T(8,128)(2,1)S(1)} %bitcast.88, bf16[256,14,128,1,1]{0,2,1,4,3:T(8,128)(2,1)S(1)} %bitcast.91), kind=kOutput, calls=%fused_computation.18 | convolution fusion | flops 3765436416 | bytes 17694720 | tf_op jit(solution)/shard_map/tfra,tjb->frajb/dot_general | solution.py:96
  278.3 18.2 %bitcast_convert_fusion.1 = bf16[16,18,128,128]{3,1,2,0:T(8,128)(2,1)} fusion(bf16[16,2,128,14,128]{4,2,3,1,0:T(8,128)(2,1)} %convolution_convert_fusion.1, s32[2,14]{1,0:T(2,128)S(1)} %multiply_add_fusion, s32[16,18]{1,0:T(8,128)S(1)} %eq.45), kind=kOutput, calls=%fused_computation.1 | convolution fusion | flops 268967808 | bytes 24118512 | tf_op jit(solution)/shard_map/fcrj,frajb->fcab/dot_general | solution.py:102
  296.5 11.0 %copy.57 = bf16[16,18,128,128]{3,2,1,0:T(8,128)(2,1)} copy(bf16[16,18,128,128]{3,1,2,0:T(8,128)(2,1)} %bitcast_convert_fusion.1) | data formatting | bytes 18874368 | tf_op jit(solution)/shard_map/convert.5
  307.5 16.8 %pad_maximum_fusion = bf16[288,128,256]{2,1,0:T(8,128)(2,1)} fusion(bf16[288,128,128]{2,1,0:T(8,128)(2,1)} %bitcast.81, bf16[288,128,128]{2,1,0:T(8,128)(2,1)} %bitcast.82), kind=kLoop, calls=%fused_computation.2 | loop fusion | flops 37748736 | bytes 37748736 | tf_op jit(solution)/shard_map/concatenate | solution.py:111
  324.4 1.1 copy-done
  325.5 9.5 %fusion.4 = f32[16,2,128,256,1]{3,2,4,1,0:T(8,128)S(1)} fusion(bf16[256,14,128,1,1]{0,2,1,4,3:T(8,128)(2,1)S(1)} %bitcast.94, bf16[16,2,14,128,128]{4,2,3,1,0:T(8,128)(2,1)} %fusion.15), kind=kOutput, calls=%fused_computation.7 | convolution fusion | flops 3758096384 | bytes 19791872 | tf_op jit(solution)/shard_map/frjab,tjb->frat/dot_general | solution.py:88
  335.0 9.6 %fusion.22 = bf16[16,2,128,256]{3,2,1,0:T(8,128)(2,1)S(1)} fusion(f32[16,2,128,256,1]{3,2,4,1,0:T(8,128)S(1)} %fusion.4, bf16[256,14,128,1,1]{0,2,1,4,3:T(8,128)(2,1)S(1)} %bitcast.92, bf16[16,2,14,128,128]{4,2,3,1,0:T(8,128)(2,1)} %fusion.12), kind=kOutput, calls=%fused_computation.20 | convolution fusion | flops 3760193536 | bytes 21889024 | tf_op jit(solution)/shard_map/frjab,tjb->frat/dot_general | solution.py:86
  344.6 3.0 copy.54
  347.6 97.7 %reduce-scatter.5.cloned.1.call-done = bf16[18,128,256]{2,1,0:T(8,128)(2,1)} async-done(((bf16[288,128,256]{2,1,0:T(8,128)(2,1)}), bf16[18,128,256]{2,1,0:T(8,128)(2,1)}) %reduce-scatter.5.cloned.1.call-update) | async-done | bytes 1179664 | tf_op jit(solution)/shard_map/reduce_scatter | solution.py:110
  445.3 2.4 fusion.38
  447.7 33.7 %reduce-scatter.3.cloned.1.call-done = bf16[512,256]{0,1:T(8,128)(2,1)} async-done(((bf16[4096,256]{0,1:T(8,128)(2,1)}), bf16[512,256]{0,1:T(8,128)(2,1)}) %reduce-scatter.3.cloned.1.call-update) | async-done | bytes 262160 | tf_op jit(solution)/shard_map/reduce_scatter | solution.py:89
  (38 shorter events, 3.6 us)
Async XLA Ops:
  7.2 81.2 %all-gather.3.cloned.1.call-start = ((), (), s32[]{:S(2)}) async-start(), calls=%async_computation.2 | async-start | bytes 10027008 | tf_op jit(solution)/shard_map/all_gather | solution.py:54
  7.9 158.0 %all-gather.5.cloned.1.call-start = ((), (), s32[]{:S(2)}) async-start(), calls=%async_computation.3 | async-start | bytes 10027008 | tf_op jit(solution)/shard_map/all_gather | solution.py:55
  8.6 436.6 %reduce-scatter.5.cloned.1.call-start = ((), (), s32[]{:S(2)}) async-start(), calls=%async_computation.5 | async-start | bytes 20054016 | tf_op jit(solution)/shard_map/reduce_scatter | solution.py:110
  9.8 7.0 %collective-permute-start = (bf16[256,512]{0,1:T(8,128)(2,1)S(1)}, bf16[256,512]{0,1:T(8,128)(2,1)S(1)}, u32[]{:S(2)}, u32[]{:S(2)}) collective-permute-start(bf16[256,512]{0,1:T(8,128)(2,1)S(1)} %copy.37), channel_id=1, source_target_pairs={{0,1},{1,2},{2,3},{3,4},{4,5},{5,6},{6,7},{7,0},{8,9},{9,10},{10,1... | collective-permute-start | bytes 786440 | tf_op jit(solution)/shard_map/ppermute | solution.py:18
  16.8 7.0 %collective-permute-start.1 = (bf16[256,512]{0,1:T(8,128)(2,1)S(1)}, bf16[256,512]{0,1:T(8,128)(2,1)S(1)}, u32[]{:S(2)}, u32[]{:S(2)}) collective-permute-start(bf16[256,512]{0,1:T(8,128)(2,1)S(1)} %collective-permute-done), channel_id=1, source_target_pairs={{0,1},{1,2},{2,3},{3,4},{4,5},{5,6},{6,7},{7,0},{8,9},{9,10},{10,1... | collective-permute-start | bytes 786440 | tf_op jit(solution)/shard_map/ppermute | solution.py:18
  23.8 7.0 %collective-permute-start.2 = (bf16[256,512]{0,1:T(8,128)(2,1)S(1)}, bf16[256,512]{0,1:T(8,128)(2,1)S(1)}, u32[]{:S(2)}, u32[]{:S(2)}) collective-permute-start(bf16[256,512]{0,1:T(8,128)(2,1)S(1)} %collective-permute-done.1), channel_id=1, source_target_pairs={{0,1},{1,2},{2,3},{3,4},{4,5},{5,6},{6,7},{7,0},{8,9},{9,10},{10,1... | collective-permute-start | bytes 786440 | tf_op jit(solution)/shard_map/ppermute | solution.py:18
  30.8 7.0 %collective-permute-start.3 = (bf16[256,512]{0,1:T(8,128)(2,1)S(1)}, bf16[256,512]{0,1:T(8,128)(2,1)S(1)}, u32[]{:S(2)}, u32[]{:S(2)}) collective-permute-start(bf16[256,512]{0,1:T(8,128)(2,1)S(1)} %collective-permute-done.2), channel_id=1, source_target_pairs={{0,1},{1,2},{2,3},{3,4},{4,5},{5,6},{6,7},{7,0},{8,9},{9,10},{10,1... | collective-permute-start | bytes 786440 | tf_op jit(solution)/shard_map/ppermute | solution.py:18
  37.8 7.0 %collective-permute-start.4 = (bf16[256,512]{0,1:T(8,128)(2,1)S(1)}, bf16[256,512]{0,1:T(8,128)(2,1)S(1)}, u32[]{:S(2)}, u32[]{:S(2)}) collective-permute-start(bf16[256,512]{0,1:T(8,128)(2,1)S(1)} %collective-permute-done.3), channel_id=1, source_target_pairs={{0,1},{1,2},{2,3},{3,4},{4,5},{5,6},{6,7},{7,0},{8,9},{9,10},{10,1... | collective-permute-start | bytes 786440 | tf_op jit(solution)/shard_map/ppermute | solution.py:18
  44.8 7.0 %collective-permute-start.5 = (bf16[256,512]{0,1:T(8,128)(2,1)S(1)}, bf16[256,512]{0,1:T(8,128)(2,1)S(1)}, u32[]{:S(2)}, u32[]{:S(2)}) collective-permute-start(bf16[256,512]{0,1:T(8,128)(2,1)S(1)} %collective-permute-done.4), channel_id=1, source_target_pairs={{0,1},{1,2},{2,3},{3,4},{4,5},{5,6},{6,7},{7,0},{8,9},{9,10},{10,1... | collective-permute-start | bytes 786440 | tf_op jit(solution)/shard_map/ppermute | solution.py:18
  51.8 7.0 %collective-permute-start.6 = (bf16[256,512]{0,1:T(8,128)(2,1)S(1)}, bf16[256,512]{0,1:T(8,128)(2,1)S(1)}, u32[]{:S(2)}, u32[]{:S(2)}) collective-permute-start(bf16[256,512]{0,1:T(8,128)(2,1)S(1)} %collective-permute-done.5), channel_id=1, source_target_pairs={{0,1},{1,2},{2,3},{3,4},{4,5},{5,6},{6,7},{7,0},{8,9},{9,10},{10,1... | collective-permute-start | bytes 786440 | tf_op jit(solution)/shard_map/ppermute | solution.py:18
  324.3 1.2 copy-start
  324.3 157.0 %reduce-scatter.3.cloned.1.call-start = ((), (), s32[]{:S(2)}) async-start(), calls=%async_computation.4 | async-start | bytes 2359296 | tf_op jit(solution)/shard_map/reduce_scatter | solution.py:89
Sparse Core Ops, SparseCore 0:
  10.2 78.1 all-gather.2
  90.6 75.2 all-gather.4
  324.5 120.7 reduce-scatter.4
  448.1 33.2 reduce-scatter.2
